TPU v7x, 512 devices: a whole 4x4x16 slice. The times are simulated.
512 devices in a mesh: vel: 16 (over y, z_hi, core), space: 32 (over x, z_lo).
Axes of the slice: x: 4, y: 4, z: 16 (z_hi: 2, z_lo: 8; z = z_hi * 8 + z_lo), core: 2. Of those that a mesh axis runs over, the one named last changes fastest.
Arguments:
- distribution: float32 [16, 256, 16, 16, 256], P('vel', 'space'), as said below
- encounter_frequency_coefficients: float32 [256, 16, 16], P('space'), may hold values from 5 to 60
Outputs:
- relaxed: float32 [16, 256, 16, 16, 256], P('vel', 'space')
Inputs may be any that keep to these rules, and one draw needn't show every extreme that they name: `distribution`: every entry is positive.
All inputs are finite; a program needn't handle non-finite values.
Results may differ from a plain program's by a relative error of at most 0.0003.
Values sent between devices are 32-bit elements; how exact they have to be, the bound alone decides.
A program may use at most 64 MiB of HBM per device.

v0:
```python
import math

import jax
import jax.numpy as jnp
from jax import lax
from jax.sharding import PartitionSpec as P

NV = 16


dv_step = 0.6
explicit_stepsize = 0.035
prandtl = 2.0 / 3.0
shear_power_law_index = 0.81
discrete_speed_points = dv_step**3 / (2.0 * math.pi) ** 1.5


def from_partner(block, axis, stride):
    count = lax.axis_size(axis)
    route = []
    for low in range(count):
        high = low | 1 << stride
        if high != low and high < count:
            route += [(low, high), (high, low)]
    return lax.ppermute(block, axis, route)


def extended(array, sides, width):
    for axis, dim in sides:
        peers, length = (lax.axis_size(axis), array.shape[dim])
        up = [(i, (i + 1) % peers) for i in range(peers)]
        down = [(j, i) for i, j in up]
        last = lax.slice_in_dim(array, length - width, length, axis=dim)
        leading = lax.slice_in_dim(array, 0, width, axis=dim)
        before = lax.ppermute(last, axis, up)
        after = lax.ppermute(leading, axis, down)
        array = jnp.concatenate([before, array, after], axis=dim)
    return array


def minmod(first, second):
    return 0.5 * (jnp.sign(first) + jnp.sign(second)) * jnp.minimum(jnp.abs(first), jnp.abs(second))


def cut(array, begin, finish, along):
    return lax.slice_in_dim(array, begin, finish, axis=along)


def divergence(padded, speed, along):
    length = padded.shape[along] - 4
    jumps = cut(padded, 1, length + 4, along) - cut(padded, 0, length + 3, along)
    slopes = minmod(cut(jumps, 0, length + 2, along), cut(jumps, 1, length + 3, along))
    center = cut(padded, 1, length + 3, along)
    upper = center + 0.5 * slopes
    lower = center - 0.5 * slopes
    fluxes = jnp.maximum(speed, 0.0) * cut(upper, 0, length + 1, along) + jnp.minimum(
        speed, 0.0
    ) * cut(lower, 1, length + 2, along)
    return cut(fluxes, 1, length + 1, along) - cut(fluxes, 0, length, along)


def central_sums(rows, flow_x, flow_y, flow_z):
    (
        particle_concentration,
        sum_x,
        sum_y,
        sum_z,
        sum_xx,
        sum_yy,
        sum_zz,
        sum_xy,
        sum_xz,
        sum_yz,
        cube_x,
        cube_y,
        cube_z,
    ) = rows
    energy = sum_xx + sum_yy + sum_zz
    flow_dot = flow_x * sum_x + flow_y * sum_y + flow_z * sum_z
    flow_sq = flow_x * flow_x + flow_y * flow_y + flow_z * flow_z
    kinetic = energy - 2.0 * flow_dot + flow_sq * particle_concentration
    tensor_x = flow_x * sum_xx + flow_y * sum_xy + flow_z * sum_xz
    tensor_y = flow_x * sum_xy + flow_y * sum_yy + flow_z * sum_yz
    tensor_z = flow_x * sum_xz + flow_y * sum_yz + flow_z * sum_zz
    flux_x = (
        cube_x
        - 2.0 * tensor_x
        - flow_x * energy
        + 2.0 * flow_x * flow_dot
        + flow_sq * sum_x
        - flow_x * flow_sq * particle_concentration
    )
    flux_y = (
        cube_y
        - 2.0 * tensor_y
        - flow_y * energy
        + 2.0 * flow_y * flow_dot
        + flow_sq * sum_y
        - flow_y * flow_sq * particle_concentration
    )
    flux_z = (
        cube_z
        - 2.0 * tensor_z
        - flow_z * energy
        + 2.0 * flow_z * flow_dot
        + flow_sq * sum_z
        - flow_z * flow_sq * particle_concentration
    )
    return jnp.stack([kinetic, flux_x, flux_y, flux_z])


def shards(distribution, encounter_frequency_coefficients):
    vz_block = distribution.shape[0]
    first_index = lax.axis_index("vel") * vz_block
    velocities = (
        (first_index + jnp.arange(vz_block)).astype(jnp.float32) - (NV - 1) / 2.0
    ) * dv_step
    speed_z = velocities.reshape(-1, 1, 1, 1, 1)
    plane_index = jnp.arange(NV * NV)
    plane_x = ((plane_index % NV).astype(jnp.float32) - (NV - 1) / 2.0) * dv_step
    plane_y = ((plane_index // NV).astype(jnp.float32) - (NV - 1) / 2.0) * dv_step
    speed_x = plane_x.reshape(1, 1, 1, 1, -1)
    speed_y = plane_y.reshape(1, 1, 1, 1, -1)
    wall_rows = distribution[:, :, :, 0:2, :]
    mirrored = wall_rows
    for bit_index in range(lax.axis_size("vel").bit_length() - 1):
        mirrored = from_partner(mirrored, "vel", bit_index)
    mirrored = mirrored[::-1]
    top_row = distribution[:, :, :, -1:, :]
    z_padded = jnp.concatenate([mirrored[:, :, :, ::-1, :], distribution, top_row, top_row], axis=3)
    y_padded = jnp.concatenate(
        [distribution[:, :, -2:], distribution, distribution[:, :, :2]], axis=2
    )
    x_padded = extended(distribution, (("space", 1),), 2)
    change = (
        divergence(x_padded, speed_x, 1)
        + divergence(y_padded, speed_y, 2)
        + divergence(z_padded, speed_z, 3)
    )
    moved = distribution - explicit_stepsize * change
    cell_shape = distribution.shape[1:4]
    cell_count = cell_shape[0] * cell_shape[1] * cell_shape[2]
    flattened = moved.reshape(vz_block, cell_count, NV * NV)
    plane_sq = plane_x * plane_x + plane_y * plane_y
    moment_table = jnp.stack(
        [
            jnp.ones_like(plane_x),
            plane_x,
            plane_y,
            plane_x * plane_x,
            plane_y * plane_y,
            plane_x * plane_y,
            plane_x * plane_sq,
            plane_y * plane_sq,
        ]
    )
    partial_value = discrete_speed_points * jnp.einsum(
        "zcp,kp->zkc", flattened, moment_table, precision=lax.Precision.HIGHEST
    )
    wall_speed = velocities.reshape(-1, 1)
    rows = (
        jnp.sum(partial_value[:, 0], axis=0),
        jnp.sum(partial_value[:, 1], axis=0),
        jnp.sum(partial_value[:, 2], axis=0),
        jnp.sum(wall_speed * partial_value[:, 0], axis=0),
        jnp.sum(partial_value[:, 3], axis=0),
        jnp.sum(partial_value[:, 4], axis=0),
        jnp.sum(wall_speed * wall_speed * partial_value[:, 0], axis=0),
        jnp.sum(partial_value[:, 5], axis=0),
        jnp.sum(wall_speed * partial_value[:, 1], axis=0),
        jnp.sum(wall_speed * partial_value[:, 2], axis=0),
        jnp.sum(partial_value[:, 6] + wall_speed * wall_speed * partial_value[:, 1], axis=0),
        jnp.sum(partial_value[:, 7] + wall_speed * wall_speed * partial_value[:, 2], axis=0),
        jnp.sum(
            wall_speed * (partial_value[:, 3] + partial_value[:, 4])
            + wall_speed * wall_speed * wall_speed * partial_value[:, 0],
            axis=0,
        ),
    )
    flow_total = lax.psum(jnp.stack(rows[0:4]), "vel")
    particle_concentration = flow_total[0]
    flow_x = flow_total[1] / particle_concentration
    flow_y = flow_total[2] / particle_concentration
    flow_z = flow_total[3] / particle_concentration
    summed_thermal_current = lax.psum(central_sums(rows, flow_x, flow_y, flow_z), "vel")
    kinetic_warmth_field = summed_thermal_current[0] / (3.0 * particle_concentration)

    def broadcast_across_grid(values):
        return values.reshape(cell_shape)[None, :, :, :, None]

    density_c = broadcast_across_grid(particle_concentration)
    shakhov_corrected_distribution = broadcast_across_grid(kinetic_warmth_field)
    rel_x = speed_x - broadcast_across_grid(flow_x)
    rel_y = speed_y - broadcast_across_grid(flow_y)
    rel_z = speed_z - broadcast_across_grid(flow_z)
    rel_sq = rel_x * rel_x + rel_y * rel_y + rel_z * rel_z
    along_heat = (
        rel_x * broadcast_across_grid(0.5 * summed_thermal_current[1])
        + rel_y * broadcast_across_grid(0.5 * summed_thermal_current[2])
        + rel_z * broadcast_across_grid(0.5 * summed_thermal_current[3])
    )
    maxwell = (
        density_c
        * shakhov_corrected_distribution ** (-1.5)
        * jnp.exp(-rel_sq / (2.0 * shakhov_corrected_distribution))
    )
    target = maxwell * (
        1.0
        + (1.0 - prandtl)
        * along_heat
        / (5.0 * density_c * shakhov_corrected_distribution * shakhov_corrected_distribution)
        * (rel_sq / shakhov_corrected_distribution - 5.0)
    )
    relaxation_multiplier = jnp.exp(
        -explicit_stepsize
        * encounter_frequency_coefficients[None, :, :, :, None]
        * density_c
        * shakhov_corrected_distribution ** (1.0 - shear_power_law_index)
    )
    return target + (moved - target) * relaxation_multiplier


def solution(mesh):
    in_specs = (P("vel", "space", None, None, None), P("space", None, None))
    out_specs = P("vel", "space", None, None, None)
    return jax.shard_map(shards, mesh=mesh, in_specs=in_specs, out_specs=out_specs, check_vma=False)
```

profile of v0, /device:TPU:4, one launch (start us, length us, event | category | flops | bytes accessed | tf_op | source)
XLA Modules:
  0.0 358.1 jit_solution(13459760709178065335)
XLA Ops:
  0.0 1.4 slice.178
  1.5 1.9 collective-permute-start.2
  3.4 2.2 fusion.62
  5.7 3.8 %collective-permute-start = (f32[1,2,16,16,256]{4,3,2,1,0:T(8,128)}, f32[1,2,16,16,256]{4,3,2,1,0:T(8,128)S(1)}, u32[]{:S(2)}, u32[]{:S(2)}) collective-permute-start(f32[1,2,16,16,256]{4,3,2,1,0:T(8,128)} %get-tuple-element.24), channel_id=1, source_target_pairs={{0,1},{1,2},{2,3},{3,4},{4,5},{5,6},{6,7},{7,8},{8,9},{9,10},{10,1... | collective-permute-start | bytes 1572872 | tf_op jit(solution)/shard_map/ppermute | solution.py:35
  9.5 11.2 %collective-permute-start.1 = (f32[1,2,16,16,256]{4,3,2,1,0:T(8,128)}, f32[1,2,16,16,256]{4,3,2,1,0:T(8,128)S(1)}, u32[]{:S(2)}, u32[]{:S(2)}) collective-permute-start(f32[1,2,16,16,256]{4,3,2,1,0:T(8,128)} %get-tuple-element.23), channel_id=1, source_target_pairs={{1,0},{2,1},{3,2},{4,3},{5,4},{6,5},{7,6},{8,7},{9,8},{10,9},{11,1... | collective-permute-start | bytes 1572872 | tf_op jit(solution)/shard_map/ppermute | solution.py:36
  21.4 1.2 copy-done.1
  22.6 1.0 multiply_multiply_fusion.2
  23.6 0.6 slice-done
  24.3 1.9 fusion.8
  26.2 0.6 fusion.53
  26.7 0.6 fusion.55
  27.3 0.6 fusion.57
  28.1 0.6 stack_broadcast_in_dim.3
  28.6 0.7 stack.6
  29.4 14.0 %collective-permute-start.3 = (f32[1,8,16,2,256]{4,2,3,1,0:T(8,128)}, f32[1,8,16,2,256]{4,2,3,1,0:T(8,128)S(1)}, u32[]{:S(2)}, u32[]{:S(2)}) collective-permute-start(f32[1,8,16,2,256]{4,2,3,1,0:T(8,128)} %collective-permute-done.2), channel_id=1, source_target_pairs={{0,64},{64,0},{32,96},{96,32},{128,192},{192,128},{160,224},{224,1... | collective-permute-start | bytes 786440 | tf_op jit(solution)/shard_map/ppermute | solution.py:25
  44.4 24.3 %collective-permute-done.3 = f32[1,8,16,2,256]{4,2,3,1,0:T(8,128)S(1)} collective-permute-done((f32[1,8,16,2,256]{4,2,3,1,0:T(8,128)}, f32[1,8,16,2,256]{4,2,3,1,0:T(8,128)S(1)}, u32[]{:S(2)}, u32[]{:S(2)}) %collective-permute-start.3) | collective-permute-done | bytes 262176 | tf_op jit(solution)/shard_map/ppermute | solution.py:25
  68.6 3.5 collective-permute-start.4
  72.1 1.2 multiply_multiply_fusion.1
  73.3 5.1 %collective-permute-done.4 = f32[1,8,16,2,256]{4,2,3,1,0:T(8,128)S(1)} collective-permute-done((f32[1,8,16,2,256]{4,2,3,1,0:T(8,128)S(1)}, f32[1,8,16,2,256]{4,2,3,1,0:T(8,128)S(1)}, u32[]{:S(2)}, u32[]{:S(2)}) %collective-permute-start.4) | collective-permute-done | bytes 262176 | tf_op jit(solution)/shard_map/ppermute | solution.py:25
  78.4 5.3 %collective-permute-start.5 = (f32[1,8,16,2,256]{4,2,3,1,0:T(8,128)S(1)}, f32[1,8,16,2,256]{4,2,3,1,0:T(8,128)S(1)}, u32[]{:S(2)}, u32[]{:S(2)}) collective-permute-start(f32[1,8,16,2,256]{4,2,3,1,0:T(8,128)S(1)} %collective-permute-done.4), channel_id=1, source_target_pairs={{0,256},{256,0},{32,288},{288,32},{64,320},{320,64},{96,352},{352,... | collective-permute-start | bytes 786440 | tf_op jit(solution)/shard_map/ppermute | solution.py:25
  83.7 2.1 fusion.5
  85.7 3.0 collective-permute-done.5
  89.0 1.0 pad_maximum_fusion.1
  90.0 2.3 multiply_multiply_fusion
  92.8 1.1 fusion.2
  94.4 0.7 copy-done.5
  95.1 1.2 fusion.28
  96.3 1.3 copy-done.2
  97.6 1.8 fusion.10
  99.5 129.6 %psum.14 = f32[4,2048]{1,0:T(4,128)S(1)} all-reduce(f32[4,2048]{1,0:T(4,128)S(1)} %pad_maximum_fusion.5), channel_id=1, replica_groups=mesh['vel'=16,'space'=32] {'vel'}, use_global_device_ids=true, to_apply=%region_0.1 | all-reduce | flops 8192 | bytes 65536 | tf_op jit(solution)/shard_map/psum | solution.py:180
  229.5 122.6 %psum.15 = f32[4,2048]{1,0:T(4,128)S(1)} all-reduce(f32[4,2048]{1,0:T(4,128)S(1)} %pad_maximum_fusion.6), channel_id=1, replica_groups=mesh['vel'=16,'space'=32] {'vel'}, use_global_device_ids=true, to_apply=%region_1.2 | all-reduce | flops 8192 | bytes 65536 | tf_op jit(solution)/shard_map/psum | solution.py:185
  353.1 5.0 %multiply_add_fusion = f32[1,8,16,16,256]{4,3,2,1,0:T(8,128)} fusion(f32[1,8,16,16,256]{4,3,2,1,0:T(8,128)S(1)} %copy-done.3, f32[8,16,16]{2,1,0:T(8,128)S(1)} %get-tuple-element.39, f32[8,16,16]{2,1,0:T(8,128)S(1)} %get-tuple-element.14, f32[8,16,16]{2,1,0:T(8,128)S(1)} %get-tuple-element.40, f32[8,16,16]{2,1,0:T(8,128)S(1)} %get-tuple-element.28, ...), kind=kLoop, calls=%fused_computation.54 | loop fusion | flops 12058624 | bytes 4286464 | tf_op jit(solution)/shard_map/add | solution.py:220
  (50 shorter events, 4.2 us)
Async XLA Ops:
  0.0 20.7 %copy-start = (f32[1,8,16,16,256]{4,3,2,1,0:T(8,128)S(1)}, f32[1,8,16,16,256]{4,3,2,1,0:T(8,128)}, u32[]{:S(2)}) copy-start(f32[1,8,16,16,256]{4,3,2,1,0:T(8,128)} %param.2) | copy-start | bytes 6291460
  1.5 27.9 %collective-permute-start.2 = (f32[1,8,16,2,256]{4,2,3,1,0:T(8,128)S(1)}, f32[1,8,16,2,256]{4,2,3,1,0:T(8,128)}, u32[]{:S(2)}, u32[]{:S(2)}) collective-permute-start(f32[1,8,16,2,256]{4,2,3,1,0:T(8,128)S(1)} %copy.6), channel_id=1, source_target_pairs={{0,32},{32,0},{64,96},{96,64},{128,160},{160,128},{192,224},{224,1... | collective-permute-start | bytes 786440 | tf_op jit(solution)/shard_map/ppermute | solution.py:25
  5.7 37.8 %collective-permute-start = (f32[1,2,16,16,256]{4,3,2,1,0:T(8,128)}, f32[1,2,16,16,256]{4,3,2,1,0:T(8,128)S(1)}, u32[]{:S(2)}, u32[]{:S(2)}) collective-permute-start(f32[1,2,16,16,256]{4,3,2,1,0:T(8,128)} %get-tuple-element.24), channel_id=1, source_target_pairs={{0,1},{1,2},{2,3},{3,4},{4,5},{5,6},{6,7},{7,8},{8,9},{9,10},{10,1... | collective-permute-start | bytes 1572872 | tf_op jit(solution)/shard_map/ppermute | solution.py:35
  9.5 34.2 %collective-permute-start.1 = (f32[1,2,16,16,256]{4,3,2,1,0:T(8,128)}, f32[1,2,16,16,256]{4,3,2,1,0:T(8,128)S(1)}, u32[]{:S(2)}, u32[]{:S(2)}) collective-permute-start(f32[1,2,16,16,256]{4,3,2,1,0:T(8,128)} %get-tuple-element.23), channel_id=1, source_target_pairs={{1,0},{2,1},{3,2},{4,3},{5,4},{6,5},{7,6},{8,7},{9,8},{10,9},{11,1... | collective-permute-start | bytes 1572872 | tf_op jit(solution)/shard_map/ppermute | solution.py:36
  21.1 1.5 copy-start.1
  22.6 1.7 slice-start
  29.4 39.2 %collective-permute-start.3 = (f32[1,8,16,2,256]{4,2,3,1,0:T(8,128)}, f32[1,8,16,2,256]{4,2,3,1,0:T(8,128)S(1)}, u32[]{:S(2)}, u32[]{:S(2)}) collective-permute-start(f32[1,8,16,2,256]{4,2,3,1,0:T(8,128)} %collective-permute-done.2), channel_id=1, source_target_pairs={{0,64},{64,0},{32,96},{96,32},{128,192},{192,128},{160,224},{224,1... | collective-permute-start | bytes 786440 | tf_op jit(solution)/shard_map/ppermute | solution.py:25
  68.6 9.8 %collective-permute-start.4 = (f32[1,8,16,2,256]{4,2,3,1,0:T(8,128)S(1)}, f32[1,8,16,2,256]{4,2,3,1,0:T(8,128)S(1)}, u32[]{:S(2)}, u32[]{:S(2)}) collective-permute-start(f32[1,8,16,2,256]{4,2,3,1,0:T(8,128)S(1)} %collective-permute-done.3), channel_id=1, source_target_pairs={{0,128},{128,0},{32,160},{160,32},{64,192},{192,64},{96,224},{224,... | collective-permute-start | bytes 786440 | tf_op jit(solution)/shard_map/ppermute | solution.py:25
  78.4 10.4 %collective-permute-start.5 = (f32[1,8,16,2,256]{4,2,3,1,0:T(8,128)S(1)}, f32[1,8,16,2,256]{4,2,3,1,0:T(8,128)S(1)}, u32[]{:S(2)}, u32[]{:S(2)}) collective-permute-start(f32[1,8,16,2,256]{4,2,3,1,0:T(8,128)S(1)} %collective-permute-done.4), channel_id=1, source_target_pairs={{0,256},{256,0},{32,288},{288,32},{64,320},{320,64},{96,352},{352,... | collective-permute-start | bytes 786440 | tf_op jit(solution)/shard_map/ppermute | solution.py:25
  92.7 1.6 copy-start.4
  92.7 2.3 copy-start.5
  96.3 1.3 copy-start.2
  96.3 256.7 %copy-start.6 = (f32[8,16,16]{2,1,0:T(8,128)S(1)}, f32[8,16,16]{2,1,0:T(8,128)}, u32[]{:S(2)}) copy-start(f32[8,16,16]{2,1,0:T(8,128)} %param.3) | copy-start | bytes 24580
  99.4 253.6 %copy-start.3 = (f32[1,8,16,16,256]{4,3,2,1,0:T(8,128)S(1)}, f32[1,8,16,16,256]{4,3,2,1,0:T(8,128)}, u32[]{:S(2)}) copy-start(f32[1,8,16,16,256]{4,3,2,1,0:T(8,128)} %copy-done.2) | copy-start | bytes 6291460
where the time goes:
time: 359 us; the launch traced here: 358 us
  blocking collectives  252 us (70%)
  starting transfers between devices  39.7 us (11%)
  waiting for transfers between devices  32.4 us (9%)
  other arithmetic  20.2 us (6%)
  local copies, waits for them, and re-layouts  11.4 us (3%)
    psum x1, blocking collectives, shards(): flow_total = lax.psum(jnp.stack(rows[0:4]), 'vel')  130 us
    psum x1, blocking collectives, shards(): lax.psum(central_sums(rows, flow_x, flow_y, flow_z), 'vel')  123 us
    ppermute x4, waiting for transfers between devices, from_partner(): return lax.ppermute(block, axis, route)  32.4 us
    ppermute x4, starting transfers between devices, from_partner(): return lax.ppermute(block, axis, route)  24.7 us
    ppermute x1, starting transfers between devices, extended(): after = lax.ppermute(leading, axis, down)  11.2 us
  transfers between devices with their start and end apart: 6, of which 3 were waited for; matrix products, arithmetic and copies ran while one was open for 4% of the time, Pallas kernels for 0%

commit v1 on v0

v1 whole, which is shorter than its diff:
```python
import functools
import math

import jax
import jax.numpy as jnp
import numpy as np
from jax import lax
from jax.experimental import pallas as pl
from jax.experimental.pallas import tpu as pltpu
from jax.sharding import PartitionSpec as P

NV = 16
UNIT = 0.3
DT = 0.035
WEIGHT = 0.6**3 / (2.0 * math.pi) ** 1.5
MESH = pl.DeviceIdType.MESH
F32 = jnp.float32
BF16 = jnp.bfloat16

HALO, WALL, SCAT, CROSS, GATH, WCROSS, WCAST, COPIES = 0, 4, 8, 16, 17, 25, 26, 34


def minmod(p, q):
    return jnp.maximum(jnp.minimum(p, q), 0.0) + jnp.minimum(jnp.maximum(p, q), 0.0)


def basis_table():
    b = np.arange(256)
    x, y = 2.0 * (b % 16) - 15, 2.0 * (b // 16) - 15
    one = np.ones(256)
    rows = [(0, one), (0, x), (0, y), (0, x * x), (0, y * y), (1, one), (1, x), (1, y), (2, one), (3, one)]
    table = np.zeros((32, 1024), np.float32)
    for part in range(3):
        for k, (block, values) in enumerate(rows):
            table[part * 10 + k, block * 256 : block * 256 + 256] = values
    return table


def cell_values(m, nu):
    mass, sx, sy, sz, xx, yy, zz, xy, xz, yz = (m[k : k + 1] for k in range(10))
    cx, cy, cz = (m[k : k + 1] + m[k + 3 : k + 4] for k in range(10, 13))
    inv = 1.0 / mass
    ux, uy, uz = sx * inv, sy * inv, sz * inv
    energy = xx + yy + zz
    dot = ux * sx + uy * sy + uz * sz
    sq = ux * ux + uy * uy + uz * uz
    kinetic = energy - 2.0 * dot + sq * mass
    common = 2.0 * dot - energy - sq * mass
    fx = cx - 2.0 * (ux * xx + uy * xy + uz * xz) + ux * common + sq * sx
    fy = cy - 2.0 * (ux * xy + uy * yy + uz * yz) + uy * common + sq * sy
    fz = cz - 2.0 * (ux * xz + uy * yz + uz * zz) + uz * common + sq * sz
    temp = (UNIT * UNIT / 3.0) * kinetic * inv
    dens = WEIGHT * mass
    log_t = jnp.log(temp)
    decay = jnp.exp(-DT * nu * dens * jnp.exp((1.0 - 0.81) * log_t))
    inv_t = 1.0 / temp
    scale = (1.0 - decay) * dens * inv_t * lax.rsqrt(temp)
    skew = (1.0 - 2.0 / 3.0) / 5.0 * (0.5 * WEIGHT * UNIT**4) * scale / dens * inv_t * inv_t
    return ux, uy, uz, (UNIT * UNIT) * inv_t, scale, skew * fx, skew * fy, skew * fz, decay


def relax(rows, basis, moved, vz):
    ux, uy, uz, rt, scale, kx, ky, kz, decay = rows
    cz = vz - uz
    coef = [
        rt * (ux * ux + uy * uy + cz * cz),
        -2.0 * rt * ux,
        -2.0 * rt * uy,
        rt,
        rt,
        kz * cz - kx * ux - ky * uy,
        kx,
        ky,
        scale,
        decay,
    ]
    coef = jnp.concatenate(coef, axis=0)
    hi = coef.astype(BF16).astype(F32)
    mid = (coef - hi).astype(BF16).astype(F32)
    low = coef - hi - mid
    stacked = jnp.concatenate([hi, mid, low, jnp.zeros((2, coef.shape[1]), F32)], axis=0)
    left = stacked.T.astype(BF16)
    wide = jnp.dot(left, basis, preferred_element_type=F32)
    rr = wide[:, 0:256]
    return jnp.exp(-0.5 * rr) * (wide[:, 512:768] + wide[:, 256:512] * (rr - 5.0)) + moved * wide[:, 768:1024]


def kernel(f_hbm, nu_ref, nuw_ref, basis_ref, out_hbm, g, acc, hp, xf, xp, ws, wr, mom, rs, zr, par, wm, wo, ws_mom, wz, wb, send, recv, local):
    vel, space = lax.axis_index("vel"), lax.axis_index("space")
    n_space = lax.axis_size("space")
    vy, zh, core = vel // 4, (vel // 2) % 2, vel % 2
    grp = vy * 2 + core

    def peer(o):
        p = (grp + o) % 8
        return {"vel": (p // 2) * 4 + zh * 2 + p % 2, "space": space}

    up = {"vel": vel, "space": (space + 1) % n_space}
    down = {"vel": vel, "space": (space + n_space - 1) % n_space}
    mirror = {"vel": NV - 1 - vel, "space": space}
    across = {"vel": vel + 2 - 4 * zh, "space": space}
    plus = vel >= NV // 2

    barrier = pltpu.get_barrier_semaphore()
    friends = [up, down, mirror, across] + [peer(o) for o in range(1, 8)]
    for d in friends:
        pl.semaphore_signal(barrier, inc=1, device_id=d, device_id_type=MESH)

    order = [0, 1, 6, 7, 2, 3, 4, 5]
    def halves(x):
        return [(f_hbm.at[x, :, pl.ds(h * 128, 128)], g.at[x, h], local.at[x, h]) for h in range(2)]

    loads = [[pltpu.make_async_copy(*c) for c in halves(x)] for x in range(8)]
    for x in order:
        for cp in loads[x]:
            cp.start()

    def remote(src, dst, k, dev):
        return pltpu.make_async_remote_copy(src, dst, send.at[k], recv.at[k], device_id=dev, device_id_type=MESH)

    vz = (2 * vel - 15).astype(F32)
    lane = lax.broadcasted_iota(jnp.int32, (8, 128), 1)
    sub = lax.broadcasted_iota(jnp.int32, (8, 128), 0)
    vx = (2 * (lane % 16) - 15).astype(F32)
    xpos = lane % 16 >= 8
    step_x = -DT * UNIT * vx
    step_y = [-DT * UNIT * (2 * (lane // 16 + 8 * h) - 15).astype(F32) for h in range(2)]

    for x in order[:4]:
        for cp in loads[x]:
            cp.wait()

    def pack(t, _):
        for h in range(2):
            near, far = pl.ds(pl.multiple_of(t * 8, 8), 8), pl.ds(pl.multiple_of(t * 8 + 128, 8), 8)
            hp[0, h, near] = jnp.where(xpos, g[6, h, near], pltpu.roll(g[6, h, far], 120, 1))
            hp[1, h, near] = jnp.where(xpos, pltpu.roll(g[1, h, far], 8, 1), g[1, h, near])
        return 0

    lax.fori_loop(0, 16, pack, 0)
    pl.semaphore_wait(barrier, len(friends))
    halo = [
        remote(g.at[7], xf.at[0], HALO, up),
        remote(g.at[0], xf.at[1], HALO + 1, down),
        remote(hp.at[0], xp.at[0], HALO + 2, up),
        remote(hp.at[1], xp.at[1], HALO + 3, down),
    ]
    for cp in halo:
        cp.start()
    for x in order[4:]:
        for cp in loads[x]:
            cp.wait()

    def pack_wall(x, _):
        for l in range(2):
            for h in range(2):
                ws[l, x, h] = g[x, h, pl.ds(l, 16, stride=16), :]
        return 0

    lax.fori_loop(0, 8, pack_wall, 0)
    wall = [remote(ws.at[0, pl.ds(4 * k, 4)], wr.at[0, pl.ds(4 * k, 4)], WALL + k, mirror) for k in range(2)]
    wall2 = [remote(ws.at[1, pl.ds(4 * k, 4)], wr.at[1, pl.ds(4 * k, 4)], WALL + 2 + k, mirror) for k in range(2)]
    for cp in wall:
        cp.start()

    @pl.when(jnp.logical_not(plus))
    def _():
        for cp in wall2:
            cp.start()

    def local_pass(positive):
        cz = -DT * UNIT * vz
        cz0 = jnp.where(sub < (2 if positive else 1), 0.0, cz)

        def body(x, _):
            for h in range(2):
                for t in range(2):
                    v = [g[x, h, k * 16 + t * 8 : k * 16 + t * 8 + 8] for k in range(16)]
                    d = [v[k] - v[k - 1] for k in range(16)]
                    half = [0.5 * minmod(d[k], d[(k + 1) % 16]) for k in range(16)]
                    if h:
                        u = [v[k] + half[k] for k in range(16)]
                        change = [u[k] - u[k - 1] for k in range(16)]
                    else:
                        u = [v[k] - half[k] for k in range(16)]
                        change = [u[(k + 1) % 16] - u[k] for k in range(16)]
                    for k in range(16):
                        acc[x, h, k * 16 + t * 8 : k * 16 + t * 8 + 8] = v[k] + step_y[h] * change[k]
                for k in range(16):
                    r0, r1 = pl.ds(k * 16, 8), pl.ds(k * 16 + 8, 8)
                    t0, t1 = g[x, h, r0], g[x, h, r1]
                    b0, b1 = pltpu.roll(t0, 1, 0), pltpu.roll(t1, 1, 0)
                    d0, d1 = t0 - b0, t1 - jnp.where(sub == 0, b0, b1)
                    a0, a1 = pltpu.roll(d0, 7, 0), pltpu.roll(d1, 7, 0)
                    m0 = 0.5 * minmod(d0, jnp.where(sub == 7, a1, a0))
                    m1 = 0.5 * minmod(d1, jnp.where(sub == 7, 0.0, a1))
                    if positive:
                        u0, u1 = t0 + m0, t1 + m1
                        s0, s1 = pltpu.roll(u0, 1, 0), pltpu.roll(u1, 1, 0)
                        e0, e1 = u0 - s0, u1 - jnp.where(sub == 0, s0, s1)
                    else:
                        u0, u1 = t0 - m0, t1 - m1
                        s0, s1 = pltpu.roll(u0, 7, 0), pltpu.roll(u1, 7, 0)
                        e0, e1 = jnp.where(sub == 7, s1, s0) - u0, jnp.where(sub == 7, t1, s1) - u1
                    acc[x, h, r0] += cz0 * e0
                    acc[x, h, r1] += cz * e1
            return 0

        lax.fori_loop(0, 8, body, 0)

    pl.when(plus)(lambda: local_pass(True))
    pl.when(jnp.logical_not(plus))(lambda: local_pass(False))

    for cp in halo:
        cp.wait_recv()

    def x_pass(t, _):
        near, far = pl.ds(pl.multiple_of(t * 8, 8), 8), pl.ds(pl.multiple_of(t * 8 + 128, 8), 8)
        for h in range(2):
            for k, rows in enumerate((near, far)):
                low, high = xp[0, h, near], xp[1, h, near]
                if k:
                    low, high = pltpu.roll(low, 8, 1), pltpu.roll(high, 120, 1)
                v = [low, xf[0, h, rows]] + [g[x, h, rows] for x in range(8)] + [xf[1, h, rows], high]
                d = [v[i + 1] - v[i] for i in range(11)]
                half = [0.5 * minmod(d[i], d[i + 1]) for i in range(10)]
                face = [jnp.where(xpos, v[i + 1] + half[i], v[i + 2] - half[i + 1]) for i in range(9)]
                for x in range(8):
                    acc[x, h, rows] += step_x * (face[x + 1] - face[x])
        return 0

    lax.fori_loop(0, 16, x_pass, 0)

    row = lax.broadcasted_iota(jnp.int32, (16, 256), 0)
    b = lax.broadcasted_iota(jnp.int32, (16, 256), 1)
    wx, wy = (2 * (b % 16) - 15).astype(F32), (2 * (b // 16) - 15).astype(F32)
    wz_ = jnp.zeros((16, 256), F32) + vz
    cube = wx * wx + wy * wy + wz_ * wz_
    table = [jnp.ones_like(wx), wx, wy, wz_, wx * wx, wy * wy, wz_ * wz_, wx * wy, wx * wz_, wy * wz_, wx * cube, wy * cube, wz_ * cube]
    weight = table[0]
    for k in range(1, 16):
        entry = table[k] if k < 13 else table[k - 3] - table[k - 3].astype(BF16).astype(F32)
        weight = jnp.where(row == k, entry, weight)
    weight = weight.astype(BF16)

    def sums(cells):
        hi = cells.astype(BF16)
        low = (cells - hi.astype(F32)).astype(BF16)
        dims = (((1,), (1,)), ((), ()))
        return lax.dot_general(weight, hi, dims, preferred_element_type=F32) + lax.dot_general(
            weight, low, dims, preferred_element_type=F32
        )

    def joined(ref, x):
        return jnp.concatenate([ref[x, 0], ref[x, 1]], axis=1)

    def main_sums(x, _):
        mom[x] = sums(joined(acc, x))
        return 0

    lax.fori_loop(0, 8, main_sums, 0)

    scatter = [remote(mom.at[(grp + o) % 8], rs.at[o], SCAT + o, peer(o)) for o in range(1, 8)]
    for cp in scatter:
        cp.start()
    total = mom[grp]
    for cp in scatter:
        cp.wait_recv()
    for o in range(1, 8):
        total = total + rs[o]
    zr[0] = total
    cross = remote(zr.at[0], zr.at[1], CROSS, across)
    cross.start()

    for cp in wall:
        cp.wait_recv()

    def wall_pass(positive):
        cz = -DT * UNIT * vz

        def body(x, _):
            for h in range(2):
                v0, v1, v2 = (g[x, h, pl.ds(l, 16, stride=16), :] for l in range(3))
                w0, d1 = wr[0, x, h], v1 - v0
                d0, m1 = v0 - w0, 0.5 * minmod(d1, v2 - v1)
                m0 = 0.5 * minmod(d0, d1)
                a0, a1 = (acc[x, h, pl.ds(l, 16, stride=16), :] for l in range(2))
                if positive:
                    bottom = w0 + 0.5 * minmod(w0 - wr[1, x, h], d0)
                    u0, u1 = v0 + m0, v1 + m1
                    a0, a1 = a0 + cz * (u0 - bottom), a1 + cz * (u1 - u0)
                else:
                    a0 = a0 + cz * ((v1 - m1) - (v0 - m0))
                wm[h, x, 0:16] = a0
                wm[h, x, 16:32] = a1
            return 0

        lax.fori_loop(0, 8, body, 0)

    @pl.when(plus)
    def _():
        for cp in wall2:
            cp.wait_recv()
        wall_pass(True)

    pl.when(jnp.logical_not(plus))(lambda: wall_pass(False))
    beside = jnp.concatenate([wm[0].reshape(256, 128), wm[1].reshape(256, 128)], axis=1)
    ws_mom[0] = sums(beside)
    wcross = remote(ws_mom.at[0], wz.at[0], WCROSS, across)
    wcross.start()

    cross.wait_recv()
    rows = cell_values(total + zr[1], nu_ref[grp])
    par[grp] = jnp.concatenate(list(rows) + [jnp.zeros((7, 256), F32)], axis=0)
    gather = [remote(par.at[grp], par.at[grp], GATH + o, peer(o)) for o in range(1, 8)]
    for cp in gather:
        cp.start()
    for cp in gather:
        cp.wait_recv()

    basis = basis_ref[...].astype(BF16)

    def main_relax(x, _):
        table = par[x]
        out = relax([table[k : k + 1] for k in range(9)], basis, joined(acc, x), vz)
        for h in range(2):
            acc[x, h] = out[:, h * 128 : h * 128 + 128]
        return 0

    lax.fori_loop(0, 8, main_relax, 0)

    wcross.wait_recv()
    wb[0] = ws_mom[0] + wz[0]
    cast = [remote(wb.at[0], wb.at[o], WCAST + o, peer(o)) for o in range(1, 8)]
    for cp in cast:
        cp.start()
    for cp in cast:
        cp.wait_recv()
    total = wb[0]
    for o in range(1, 8):
        total = total + wb[o]
    out = relax(cell_values(total, nuw_ref[...]), basis, beside, vz)
    for h in range(2):
        wo[h] = out[:, h * 128 : h * 128 + 128].reshape(8, 32, 128)

    def place(x, _):
        for l in range(2):
            for h in range(2):
                acc[x, h, pl.ds(l, 16, stride=16), :] = wo[h, x, l * 16 : l * 16 + 16]
        return 0

    lax.fori_loop(0, 8, place, 0)
    stores = [
        pltpu.make_async_copy(acc.at[x, h], out_hbm.at[x, :, pl.ds(h * 128, 128)], local.at[x, h])
        for x in range(8)
        for h in range(2)
    ]
    for cp in stores:
        cp.start()
    for cp in halo + wall + scatter + [cross, wcross] + gather + cast:
        cp.wait_send()

    @pl.when(jnp.logical_not(plus))
    def _():
        for cp in wall2:
            cp.wait_send()

    for cp in stores:
        cp.wait()


def shards(distribution, coefficients):
    cells = distribution.reshape(8, 256, 256)
    nu = coefficients.reshape(8, 1, 256)
    nu_wall = coefficients[:, :, 0:2].transpose(0, 2, 1).reshape(1, 256)
    vmem, anywhere = pl.BlockSpec(memory_space=pltpu.VMEM), pl.BlockSpec(memory_space=pl.ANY)
    out = pl.pallas_call(
        kernel,
        out_shape=jax.ShapeDtypeStruct((8, 256, 256), F32),
        in_specs=[anywhere, vmem, vmem, vmem],
        out_specs=anywhere,
        scratch_shapes=[
            pltpu.VMEM((8, 2, 256, 128), F32),
            pltpu.VMEM((8, 2, 256, 128), F32),
            pltpu.VMEM((2, 2, 128, 128), F32),
            pltpu.VMEM((2, 2, 256, 128), F32),
            pltpu.VMEM((2, 2, 128, 128), F32),
            pltpu.VMEM((2, 8, 2, 16, 128), F32),
            pltpu.VMEM((2, 8, 2, 16, 128), F32),
            pltpu.VMEM((8, 16, 256), F32),
            pltpu.VMEM((8, 16, 256), F32),
            pltpu.VMEM((2, 16, 256), F32),
            pltpu.VMEM((8, 16, 256), F32),
            pltpu.VMEM((2, 8, 32, 128), F32),
            pltpu.VMEM((2, 8, 32, 128), F32),
            pltpu.VMEM((1, 16, 256), F32),
            pltpu.VMEM((1, 16, 256), F32),
            pltpu.VMEM((8, 16, 256), F32),
            pltpu.SemaphoreType.DMA((COPIES,)),
            pltpu.SemaphoreType.DMA((COPIES,)),
            pltpu.SemaphoreType.DMA((8, 2)),
        ],
        compiler_params=pltpu.CompilerParams(
            collective_id=0, has_side_effects=True, vmem_limit_bytes=40 * 1024 * 1024
        ),
        cost_estimate=pl.CostEstimate(flops=10**8, bytes_accessed=4 * 2**20, transcendentals=2**19),
    )(cells, nu, nu_wall, jnp.asarray(basis_table()))
    return out.reshape(distribution.shape)


def solution(mesh):
    in_specs = (P("vel", "space", None, None, None), P("space", None, None))
    out_specs = P("vel", "space", None, None, None)
    return jax.shard_map(shards, mesh=mesh, in_specs=in_specs, out_specs=out_specs, check_vma=False)
```

time: 359 us -> 85.8 us (0.24)
  the two profiles are of different devices: /device:TPU:4 before, /device:TPU:1 now
where the time goes in v1:
time: 85.8 us; the launch traced here: 85.6 us
  Pallas kernels  79.8 us (93%)
  local copies, waits for them, and re-layouts  5.81 us (7%)
    pallas_call x1, Pallas kernels, shards(): pl.pallas_call(kernel, out_shape=jax.ShapeDtypeStruct((8, 256, 256), F32)...  79.8 us
    unnamed x5, local copies, waits for them, and re-layouts  3.83 us

profile of v1, /device:TPU:1, one launch (start us, length us, event | category | flops | bytes accessed | tf_op | source)
XLA Modules:
  0.0 85.6 jit_solution(14060530830991869439)
XLA Ops:
  0.0 0.9 %reshape.13.nu_ref = f32[8,1,256]{2,1,0:T(1,128)S(1)} reshape(f32[8,16,16]{2,1,0:T(8,128)} %param.4) | data formatting | bytes 16384 | tf_op jit(solution)/shard_map/reshape | solution.py:374
  0.9 0.8 slice_bitcast_fusion
  1.8 0.1 copy.4
  1.9 0.1 reshape.14.nuw_ref
  2.0 0.0 copy-start
  2.0 1.6 %copy-done = f32[1,8,16,16,256]{4,3,2,1,0:T(8,128)S(1)} copy-done((f32[1,8,16,16,256]{4,3,2,1,0:T(8,128)S(1)}, f32[1,8,16,16,256]{4,3,2,1,0:T(8,128)}, u32[]{:S(2)}) %copy-start) | copy-done | bytes 2097176
  3.6 0.0 copy-start.1
  3.6 0.9 %copy-done.1 = f32[32,1024]{1,0:T(8,128)S(1)} copy-done((f32[32,1024]{1,0:T(8,128)S(1)}, f32[32,1024]{1,0:T(8,128)}, u32[]{:S(2)}) %copy-start.1) | copy-done | bytes 131096
  4.5 79.8 %shard_map.37 = f32[8,256,256]{2,1,0:T(8,128)S(1)} custom-call(f32[8,256,256]{2,1,0:T(8,128)S(1)} %bitcast.5, f32[8,1,256]{2,1,0:T(1,128)S(1)} %reshape.13.nu_ref, f32[1,256]{1,0:T(1,128)S(1)} %reshape.14.nuw_ref, f32[32,1024]{1,0:T(8,128)S(1)} %copy-done.1), custom_call_target="tpu_custom_call" | custom-call | flops 100000000 | bytes 4194304 | tf_op jit(solution)/shard_map/pallas_call | solution.py:377
  84.3 1.3 %copy.6 = f32[1,8,16,16,256]{4,3,2,1,0:T(8,128)} copy(f32[1,8,16,16,256]{4,3,2,1,0:T(8,128)S(1)} %bitcast.4) | data formatting | bytes 4194304
Async XLA Ops:
  2.0 1.6 %copy-start = (f32[1,8,16,16,256]{4,3,2,1,0:T(8,128)S(1)}, f32[1,8,16,16,256]{4,3,2,1,0:T(8,128)}, u32[]{:S(2)}) copy-start(f32[1,8,16,16,256]{4,3,2,1,0:T(8,128)} %param.3) | copy-start | bytes 6291460
  3.6 0.9 %copy-start.1 = (f32[32,1024]{1,0:T(8,128)S(1)}, f32[32,1024]{1,0:T(8,128)}, u32[]{:S(2)}) copy-start(f32[32,1024]{1,0:T(8,128)} %constant.2.clone.basis_ref) | copy-start | bytes 393220

commit v2 on v1

--- a/solution.py
+++ b/solution.py
@@ -1,9 +1,7 @@
-import functools
 import math
 
 import jax
 import jax.numpy as jnp
-import numpy as np
 from jax import lax
 from jax.experimental import pallas as pl
 from jax.experimental.pallas import tpu as pltpu
@@ -17,7 +15,7 @@
 F32 = jnp.float32
 BF16 = jnp.bfloat16
 
-HALO, WALL, SCAT, CROSS, GATH, WCROSS, WCAST, COPIES = 0, 4, 8, 16, 17, 25, 26, 34
+HALO, WALL, SCAT, CROSS, GATH, PRE, CAST, COPIES = 0, 4, 8, 16, 17, 25, 26, 34
 
 
 def minmod(p, q):
@@ -25,15 +23,54 @@
 
 
 def basis_table():
-    b = np.arange(256)
-    x, y = 2.0 * (b % 16) - 15, 2.0 * (b // 16) - 15
-    one = np.ones(256)
-    rows = [(0, one), (0, x), (0, y), (0, x * x), (0, y * y), (1, one), (1, x), (1, y), (2, one), (3, one)]
-    table = np.zeros((32, 1024), np.float32)
-    for part in range(3):
-        for k, (block, values) in enumerate(rows):
-            table[part * 10 + k, block * 256 : block * 256 + 256] = values
-    return table
+    row = lax.broadcasted_iota(jnp.int32, (32, 1024), 0)
+    col = lax.broadcasted_iota(jnp.int32, (32, 1024), 1)
+    b, block, k = col % 256, col // 256, row % 10
+    x, y = (2 * (b % 16) - 15).astype(F32), (2 * (b // 16) - 15).astype(F32)
+    value = jnp.where((k == 1) | (k == 6), x, 1.0)
+    value = jnp.where((k == 2) | (k == 7), y, value)
+    value = jnp.where(k == 3, x * x, jnp.where(k == 4, y * y, value))
+    wanted = jnp.where(k < 5, 0, jnp.where(k < 8, 1, k - 6))
+    return jnp.where((block == wanted) & (row < 30), value, 0.0).astype(BF16)
+
+
+def spread(tile, width):
+    k, c = (lax.broadcasted_iota(jnp.int32, (16, 256), d) for d in range(2))
+    pick = jnp.where(c % width == k, 1.0, 0.0)
+    wide = jnp.dot(tile, pick, precision=lax.Precision.HIGHEST, preferred_element_type=F32)
+    r, c = (lax.broadcasted_iota(jnp.int32, wide.shape, d) for d in range(2))
+    return jnp.sum(jnp.where(r == c // width, wide, 0.0), axis=0, keepdims=True)
+
+
+def sum_weights(vz):
+    row = lax.broadcasted_iota(jnp.int32, (16, 256), 0)
+    b = lax.broadcasted_iota(jnp.int32, (16, 256), 1)
+    x, y = (2 * (b % 16) - 15).astype(F32), (2 * (b // 16) - 15).astype(F32)
+    z = jnp.zeros((16, 256), F32) + vz
+    sq = x * x + y * y + z * z
+    table = [jnp.ones_like(x), x, y, z, x * x, y * y, z * z, x * y, x * z, y * z, x * sq, y * sq, z * sq]
+    weight = table[0]
+    for k in range(1, 16):
+        entry = table[k] if k < 13 else table[k - 3] - table[k - 3].astype(BF16).astype(F32)
+        weight = jnp.where(row == k, entry, weight)
+    return weight.astype(BF16)
+
+
+def sums(weight, cells):
+    hi = cells.astype(BF16)
+    low = (cells - hi.astype(F32)).astype(BF16)
+    dims = (((1,), (1,)), ((), ()))
+    return lax.dot_general(weight, hi, dims, preferred_element_type=F32) + lax.dot_general(
+        weight, low, dims, preferred_element_type=F32
+    )
+
+
+def joined(ref, x):
+    return jnp.concatenate([ref[x, 0], ref[x, 1]], axis=1)
+
+
+def flat(ref):
+    return jnp.concatenate([ref[0].reshape(256, 128), ref[1].reshape(256, 128)], axis=1)
 
 
 def cell_values(m, nu):
@@ -85,7 +122,7 @@
     return jnp.exp(-0.5 * rr) * (wide[:, 512:768] + wide[:, 256:512] * (rr - 5.0)) + moved * wide[:, 768:1024]
 
 
-def kernel(f_hbm, nu_ref, nuw_ref, basis_ref, out_hbm, g, acc, hp, xf, xp, ws, wr, mom, rs, zr, par, wm, wo, ws_mom, wz, wb, send, recv, local):
+def kernel(f_hbm, nu_hbm, out, g, acc, nu, hp, xf, xp, ws, wr, mom, rs, zr, par, wm, dp, dm, pre, cast, send, recv, local, nu_sem):
     vel, space = lax.axis_index("vel"), lax.axis_index("space")
     n_space = lax.axis_size("space")
     vy, zh, core = vel // 4, (vel // 2) % 2, vel % 2
@@ -114,6 +151,9 @@
     for x in order:
         for cp in loads[x]:
             cp.start()
+
+    load_nu = pltpu.make_async_copy(nu_hbm, nu, nu_sem)
+    load_nu.start()
 
     def remote(src, dst, k, dev):
         return pltpu.make_async_remote_copy(src, dst, send.at[k], recv.at[k], device_id=dev, device_id_type=MESH)
@@ -158,19 +198,13 @@
         return 0
 
     lax.fori_loop(0, 8, pack_wall, 0)
-    wall = [remote(ws.at[0, pl.ds(4 * k, 4)], wr.at[0, pl.ds(4 * k, 4)], WALL + k, mirror) for k in range(2)]
-    wall2 = [remote(ws.at[1, pl.ds(4 * k, 4)], wr.at[1, pl.ds(4 * k, 4)], WALL + 2 + k, mirror) for k in range(2)]
+    wall = [remote(ws.at[l], wr.at[l], WALL + l, mirror) for l in range(2)]
     for cp in wall:
         cp.start()
 
-    @pl.when(jnp.logical_not(plus))
-    def _():
-        for cp in wall2:
-            cp.start()
-
     def local_pass(positive):
         cz = -DT * UNIT * vz
-        cz0 = jnp.where(sub < (2 if positive else 1), 0.0, cz)
+        cz0 = jnp.where(sub < 1, 0.0, cz) if positive else cz
 
         def body(x, _):
             for h in range(2):
@@ -197,11 +231,11 @@
                     if positive:
                         u0, u1 = t0 + m0, t1 + m1
                         s0, s1 = pltpu.roll(u0, 1, 0), pltpu.roll(u1, 1, 0)
-                        e0, e1 = u0 - s0, u1 - jnp.where(sub == 0, s0, s1)
+                        e0, e1 = u0 - jnp.where(sub < 2, 0.0, s0), u1 - jnp.where(sub == 0, s0, s1)
                     else:
                         u0, u1 = t0 - m0, t1 - m1
                         s0, s1 = pltpu.roll(u0, 7, 0), pltpu.roll(u1, 7, 0)
-                        e0, e1 = jnp.where(sub == 7, s1, s0) - u0, jnp.where(sub == 7, t1, s1) - u1
+                        e0, e1 = jnp.where(sub == 7, s1, s0) - jnp.where(sub == 0, 0.0, u0), jnp.where(sub == 7, t1, s1) - u1
                     acc[x, h, r0] += cz0 * e0
                     acc[x, h, r1] += cz * e1
             return 0
@@ -231,31 +265,10 @@
 
     lax.fori_loop(0, 16, x_pass, 0)
 
-    row = lax.broadcasted_iota(jnp.int32, (16, 256), 0)
-    b = lax.broadcasted_iota(jnp.int32, (16, 256), 1)
-    wx, wy = (2 * (b % 16) - 15).astype(F32), (2 * (b // 16) - 15).astype(F32)
-    wz_ = jnp.zeros((16, 256), F32) + vz
-    cube = wx * wx + wy * wy + wz_ * wz_
-    table = [jnp.ones_like(wx), wx, wy, wz_, wx * wx, wy * wy, wz_ * wz_, wx * wy, wx * wz_, wy * wz_, wx * cube, wy * cube, wz_ * cube]
-    weight = table[0]
-    for k in range(1, 16):
-        entry = table[k] if k < 13 else table[k - 3] - table[k - 3].astype(BF16).astype(F32)
-        weight = jnp.where(row == k, entry, weight)
-    weight = weight.astype(BF16)
-
-    def sums(cells):
-        hi = cells.astype(BF16)
-        low = (cells - hi.astype(F32)).astype(BF16)
-        dims = (((1,), (1,)), ((), ()))
-        return lax.dot_general(weight, hi, dims, preferred_element_type=F32) + lax.dot_general(
-            weight, low, dims, preferred_element_type=F32
-        )
-
-    def joined(ref, x):
-        return jnp.concatenate([ref[x, 0], ref[x, 1]], axis=1)
+    weight = sum_weights(vz)
 
     def main_sums(x, _):
-        mom[x] = sums(joined(acc, x))
+        mom[x] = sums(weight, joined(acc, x))
         return 0
 
     lax.fori_loop(0, 8, main_sums, 0)
@@ -263,6 +276,22 @@
     scatter = [remote(mom.at[(grp + o) % 8], rs.at[o], SCAT + o, peer(o)) for o in range(1, 8)]
     for cp in scatter:
         cp.start()
+
+    def gather_wall(x, _):
+        for l in range(2):
+            for h in range(2):
+                wm[h, x, pl.ds(l, 16, stride=2), :] = acc[x, h, pl.ds(l, 16, stride=16), :]
+        return 0
+
+    lax.fori_loop(0, 8, gather_wall, 0)
+    pre[0] = sums(weight, flat(wm))
+    early = remote(pre.at[0], pre.at[1], PRE, mirror)
+    early.start()
+    load_nu.wait()
+    nu_main = spread(nu[grp], 16)
+    nu_wall = spread(nu[...].reshape(128, 16), 2)
+    basis = basis_table()
+
     total = mom[grp]
     for cp in scatter:
         cp.wait_recv()
@@ -272,116 +301,75 @@
     cross = remote(zr.at[0], zr.at[1], CROSS, across)
     cross.start()
 
-    for cp in wall:
-        cp.wait_recv()
-
-    def wall_pass(positive):
-        cz = -DT * UNIT * vz
-
-        def body(x, _):
-            for h in range(2):
-                v0, v1, v2 = (g[x, h, pl.ds(l, 16, stride=16), :] for l in range(3))
-                w0, d1 = wr[0, x, h], v1 - v0
-                d0, m1 = v0 - w0, 0.5 * minmod(d1, v2 - v1)
-                m0 = 0.5 * minmod(d0, d1)
-                a0, a1 = (acc[x, h, pl.ds(l, 16, stride=16), :] for l in range(2))
-                if positive:
-                    bottom = w0 + 0.5 * minmod(w0 - wr[1, x, h], d0)
-                    u0, u1 = v0 + m0, v1 + m1
-                    a0, a1 = a0 + cz * (u0 - bottom), a1 + cz * (u1 - u0)
-                else:
-                    a0 = a0 + cz * ((v1 - m1) - (v0 - m0))
-                wm[h, x, 0:16] = a0
-                wm[h, x, 16:32] = a1
-            return 0
-
-        lax.fori_loop(0, 8, body, 0)
-
-    @pl.when(plus)
-    def _():
-        for cp in wall2:
-            cp.wait_recv()
-        wall_pass(True)
-
-    pl.when(jnp.logical_not(plus))(lambda: wall_pass(False))
-    beside = jnp.concatenate([wm[0].reshape(256, 128), wm[1].reshape(256, 128)], axis=1)
-    ws_mom[0] = sums(beside)
-    wcross = remote(ws_mom.at[0], wz.at[0], WCROSS, across)
-    wcross.start()
-
     cross.wait_recv()
-    rows = cell_values(total + zr[1], nu_ref[grp])
+    rows = cell_values(total + zr[1], nu_main)
     par[grp] = jnp.concatenate(list(rows) + [jnp.zeros((7, 256), F32)], axis=0)
     gather = [remote(par.at[grp], par.at[grp], GATH + o, peer(o)) for o in range(1, 8)]
     for cp in gather:
         cp.start()
+    for cp in wall:
+        cp.wait_recv()
+    step_wall = -DT * UNIT * jnp.abs(vz)
+
+    def wall_pass(x, _):
+        for h in range(2):
+            v0, v1 = (g[x, h, pl.ds(l, 16, stride=16), :] for l in range(2))
+            w0, w1 = wr[0, x, h], wr[1, x, h]
+            p0, p1, m0, m1 = (jnp.where(plus, a, b) for a, b in ((v0, w0), (v1, w1), (w0, v0), (w1, v1)))
+            jump = p0 - m0
+            into = step_wall * (m0 - 0.5 * minmod(m1 - m0, -jump))
+            out_of = step_wall * (p0 + 0.5 * minmod(jump, p1 - p0))
+            dp[h, x, pl.ds(0, 16, stride=2), :] = out_of - into
+            dp[h, x, pl.ds(1, 16, stride=2), :] = -out_of
+            dm[h, x, pl.ds(0, 16, stride=2), :] = into
+            dm[h, x, pl.ds(1, 16, stride=2), :] = jnp.zeros_like(into)
+        return 0
+
+    lax.fori_loop(0, 8, wall_pass, 0)
+    plus_part, minus_part = flat(dp), flat(dm)
+    early.wait_recv()
+    part = sums(sum_weights(jnp.abs(vz)), plus_part) + sums(sum_weights(-jnp.abs(vz)), minus_part)
+    cast[0] = part + (pre[0] + pre[1])
+    casts = [remote(cast.at[0], cast.at[o], CAST + o, peer(o)) for o in range(1, 8)]
+    for cp in casts:
+        cp.start()
+    beside = flat(wm) + jnp.where(plus, plus_part, minus_part)
+
     for cp in gather:
         cp.wait_recv()
 
-    basis = basis_ref[...].astype(BF16)
-
     def main_relax(x, _):
         table = par[x]
-        out = relax([table[k : k + 1] for k in range(9)], basis, joined(acc, x), vz)
-        for h in range(2):
-            acc[x, h] = out[:, h * 128 : h * 128 + 128]
+        out[x] = relax([table[k : k + 1] for k in range(9)], basis, joined(acc, x), vz)
         return 0
 
     lax.fori_loop(0, 8, main_relax, 0)
 
-    wcross.wait_recv()
-    wb[0] = ws_mom[0] + wz[0]
-    cast = [remote(wb.at[0], wb.at[o], WCAST + o, peer(o)) for o in range(1, 8)]
-    for cp in cast:
-        cp.start()
-    for cp in cast:
+    for cp in casts:
         cp.wait_recv()
-    total = wb[0]
+    total = cast[0]
     for o in range(1, 8):
-        total = total + wb[o]
-    out = relax(cell_values(total, nuw_ref[...]), basis, beside, vz)
-    for h in range(2):
-        wo[h] = out[:, h * 128 : h * 128 + 128].reshape(8, 32, 128)
-
-    def place(x, _):
-        for l in range(2):
-            for h in range(2):
-                acc[x, h, pl.ds(l, 16, stride=16), :] = wo[h, x, l * 16 : l * 16 + 16]
-        return 0
-
-    lax.fori_loop(0, 8, place, 0)
-    stores = [
-        pltpu.make_async_copy(acc.at[x, h], out_hbm.at[x, :, pl.ds(h * 128, 128)], local.at[x, h])
-        for x in range(8)
-        for h in range(2)
-    ]
-    for cp in stores:
-        cp.start()
-    for cp in halo + wall + scatter + [cross, wcross] + gather + cast:
+        total = total + cast[o]
+    fixed = relax(cell_values(total, nu_wall), basis, beside, vz)
+    for x in range(8):
+        for k in range(16):
+            out[x, k * 16 : k * 16 + 2, :] = fixed[x * 32 + k * 2 : x * 32 + k * 2 + 2]
+    for cp in halo + wall + scatter + [cross, early] + gather + casts:
         cp.wait_send()
-
-    @pl.when(jnp.logical_not(plus))
-    def _():
-        for cp in wall2:
-            cp.wait_send()
-
-    for cp in stores:
-        cp.wait()
 
 
 def shards(distribution, coefficients):
     cells = distribution.reshape(8, 256, 256)
-    nu = coefficients.reshape(8, 1, 256)
-    nu_wall = coefficients[:, :, 0:2].transpose(0, 2, 1).reshape(1, 256)
-    vmem, anywhere = pl.BlockSpec(memory_space=pltpu.VMEM), pl.BlockSpec(memory_space=pl.ANY)
+    hbm = pl.BlockSpec(memory_space=pltpu.HBM)
     out = pl.pallas_call(
         kernel,
         out_shape=jax.ShapeDtypeStruct((8, 256, 256), F32),
-        in_specs=[anywhere, vmem, vmem, vmem],
-        out_specs=anywhere,
+        in_specs=[hbm, hbm],
+        out_specs=pl.BlockSpec(memory_space=pltpu.VMEM),
         scratch_shapes=[
             pltpu.VMEM((8, 2, 256, 128), F32),
             pltpu.VMEM((8, 2, 256, 128), F32),
+            pltpu.VMEM((8, 16, 16), F32),
             pltpu.VMEM((2, 2, 128, 128), F32),
             pltpu.VMEM((2, 2, 256, 128), F32),
             pltpu.VMEM((2, 2, 128, 128), F32),
@@ -393,18 +381,19 @@
             pltpu.VMEM((8, 16, 256), F32),
             pltpu.VMEM((2, 8, 32, 128), F32),
             pltpu.VMEM((2, 8, 32, 128), F32),
-            pltpu.VMEM((1, 16, 256), F32),
-            pltpu.VMEM((1, 16, 256), F32),
+            pltpu.VMEM((2, 8, 32, 128), F32),
+            pltpu.VMEM((2, 16, 256), F32),
             pltpu.VMEM((8, 16, 256), F32),
             pltpu.SemaphoreType.DMA((COPIES,)),
             pltpu.SemaphoreType.DMA((COPIES,)),
             pltpu.SemaphoreType.DMA((8, 2)),
+            pltpu.SemaphoreType.DMA,
         ],
         compiler_params=pltpu.CompilerParams(
             collective_id=0, has_side_effects=True, vmem_limit_bytes=40 * 1024 * 1024
         ),
         cost_estimate=pl.CostEstimate(flops=10**8, bytes_accessed=4 * 2**20, transcendentals=2**19),
-    )(cells, nu, nu_wall, jnp.asarray(basis_table()))
+    )(pltpu.with_memory_space_constraint(cells, pltpu.HBM), pltpu.with_memory_space_constraint(coefficients, pltpu.HBM))
     return out.reshape(distribution.shape)
 
 

time: 85.8 us -> 75 us (0.87)
  Pallas kernels: 79.8 us -> 73.5 us
  local copies, waits for them, and re-layouts: 5.81 us -> 1.32 us
    pallas_call x1, Pallas kernels: 79.8 us -> 73.5 us  [shards(): pl.pallas_call(kernel, out_shape=jax.ShapeDtypeStruct((8, 256, 256), F32)...]
    unnamed x5 -> x1, local copies, waits for them, and re-layouts: 3.83 us -> 1.32 us
    reshape x2 -> x0, local copies, waits for them, and re-layouts: 1.02 us -> none  [the longest x1 0.93 us: shards(): nu = coefficients.reshape(8, 1, 256)]
    transpose x2 -> x0, local copies, waits for them, and re-layouts: 0.96 us -> none  [shards(): nu_wall = coefficients[:, :, 0:2].transpose(0, 2, 1).reshape(1, 256)]
where the time goes in v2:
time: 75 us; the launch traced here: 74.9 us
  Pallas kernels  73.5 us (98%)
  local copies, waits for them, and re-layouts  1.32 us (2%)
    pallas_call x1, Pallas kernels, shards(): pl.pallas_call(kernel, out_shape=jax.ShapeDtypeStruct((8, 256, 256), F32)...  73.5 us

profile of v2, /device:TPU:1, one launch (start us, length us, event | category | flops | bytes accessed | tf_op | source)
XLA Modules:
  0.0 74.9 jit_solution(7078708415634997700)
XLA Ops:
  0.0 73.5 %shard_map.28 = f32[8,256,256]{2,1,0:T(8,128)S(1)} custom-call(f32[8,256,256]{2,1,0:T(8,128)} %bitcast.3, f32[8,16,16]{2,1,0:T(8,128)} %nu_hbm.1), custom_call_target="tpu_custom_call" | custom-call | flops 100000000 | bytes 4194304 | tf_op jit(solution)/shard_map/pallas_call | solution.py:364
  73.6 1.3 %copy.4 = f32[1,8,16,16,256]{4,3,2,1,0:T(8,128)} copy(f32[1,8,16,16,256]{4,3,2,1,0:T(8,128)S(1)} %bitcast.2) | data formatting | bytes 4194304

commit v3 on v2

--- a/solution.py
+++ b/solution.py
@@ -15,7 +15,7 @@
 F32 = jnp.float32
 BF16 = jnp.bfloat16
 
-HALO, WALL, SCAT, CROSS, GATH, PRE, CAST, COPIES = 0, 4, 8, 16, 17, 25, 26, 34
+HALO, WALL, SCAT, CROSS, GATH, CAST, COPIES = 0, 4, 8, 16, 17, 25, 33
 
 
 def minmod(p, q):
@@ -74,8 +74,8 @@
 
 
 def cell_values(m, nu):
-    mass, sx, sy, sz, xx, yy, zz, xy, xz, yz = (m[k : k + 1] for k in range(10))
-    cx, cy, cz = (m[k : k + 1] + m[k + 3 : k + 4] for k in range(10, 13))
+    mass, sx, sy, sz, xx, yy, zz, xy, xz, yz = m[:10]
+    cx, cy, cz = (m[k] + m[k + 3] for k in range(10, 13))
     inv = 1.0 / mass
     ux, uy, uz = sx * inv, sy * inv, sz * inv
     energy = xx + yy + zz
@@ -122,7 +122,7 @@
     return jnp.exp(-0.5 * rr) * (wide[:, 512:768] + wide[:, 256:512] * (rr - 5.0)) + moved * wide[:, 768:1024]
 
 
-def kernel(f_hbm, nu_hbm, out, g, acc, nu, hp, xf, xp, ws, wr, mom, rs, zr, par, wm, dp, dm, pre, cast, send, recv, local, nu_sem):
+def kernel(f_hbm, nu_hbm, out, g, acc, nu, hp, xf, xp, ws, wr, mom, rs, zr, par, vals, freq, wm, dp, dm, cast, send, recv, local, nu_sem):
     vel, space = lax.axis_index("vel"), lax.axis_index("space")
     n_space = lax.axis_size("space")
     vy, zh, core = vel // 4, (vel // 2) % 2, vel % 2
@@ -181,8 +181,8 @@
     pl.semaphore_wait(barrier, len(friends))
     halo = [
         remote(g.at[7], xf.at[0], HALO, up),
+        remote(hp.at[0], xp.at[0], HALO + 2, up),
         remote(g.at[0], xf.at[1], HALO + 1, down),
-        remote(hp.at[0], xp.at[0], HALO + 2, up),
         remote(hp.at[1], xp.at[1], HALO + 3, down),
     ]
     for cp in halo:
@@ -199,8 +199,13 @@
 
     lax.fori_loop(0, 8, pack_wall, 0)
     wall = [remote(ws.at[l], wr.at[l], WALL + l, mirror) for l in range(2)]
-    for cp in wall:
-        cp.start()
+    late = (space % 8 >= 3) & (space % 8 <= 4)
+
+    def start_wall():
+        for cp in wall:
+            cp.start()
+
+    pl.when(jnp.logical_not(late))(start_wall)
 
     def local_pass(positive):
         cz = -DT * UNIT * vz
@@ -245,33 +250,56 @@
     pl.when(plus)(lambda: local_pass(True))
     pl.when(jnp.logical_not(plus))(lambda: local_pass(False))
 
+    def x_inner(t, _):
+        rows = pl.ds(pl.multiple_of(t * 8, 8), 8)
+        for h in range(2):
+            v = [g[x, h, rows] for x in range(8)]
+            d = [v[i + 1] - v[i] for i in range(7)]
+            half = [0.5 * minmod(d[i], d[i + 1]) for i in range(6)]
+            face = [jnp.where(xpos, v[i + 1] + half[i], v[i + 2] - half[i + 1]) for i in range(5)]
+            for x in range(4):
+                acc[x + 2, h, rows] += step_x * (face[x + 1] - face[x])
+        return 0
+
+    lax.fori_loop(0, 32, x_inner, 0)
+    weight = sum_weights(vz)
+
+    def layer_sums(x):
+        mom[x] = sums(weight, joined(acc, x))
+
+    lax.fori_loop(2, 6, lambda x, _: (layer_sums(x), 0)[1], 0)
+    load_nu.wait()
+
+    def frequencies(x, _):
+        freq[pl.ds(x, 1), :] = spread(nu[x], 16)
+        return 0
+
+    lax.fori_loop(0, 8, frequencies, 0)
+    nu_wall = spread(nu[...].reshape(128, 16), 2)
+    basis = basis_table()
+
     for cp in halo:
         cp.wait_recv()
 
-    def x_pass(t, _):
+    def x_outer(t, _):
         near, far = pl.ds(pl.multiple_of(t * 8, 8), 8), pl.ds(pl.multiple_of(t * 8 + 128, 8), 8)
         for h in range(2):
             for k, rows in enumerate((near, far)):
                 low, high = xp[0, h, near], xp[1, h, near]
                 if k:
                     low, high = pltpu.roll(low, 8, 1), pltpu.roll(high, 120, 1)
-                v = [low, xf[0, h, rows]] + [g[x, h, rows] for x in range(8)] + [xf[1, h, rows], high]
-                d = [v[i + 1] - v[i] for i in range(11)]
-                half = [0.5 * minmod(d[i], d[i + 1]) for i in range(10)]
-                face = [jnp.where(xpos, v[i + 1] + half[i], v[i + 2] - half[i + 1]) for i in range(9)]
-                for x in range(8):
-                    acc[x, h, rows] += step_x * (face[x + 1] - face[x])
-        return 0
-
-    lax.fori_loop(0, 16, x_pass, 0)
-
-    weight = sum_weights(vz)
-
-    def main_sums(x, _):
-        mom[x] = sums(weight, joined(acc, x))
-        return 0
-
-    lax.fori_loop(0, 8, main_sums, 0)
+                below = [low, xf[0, h, rows]] + [g[x, h, rows] for x in range(4)]
+                above = [g[x, h, rows] for x in range(4, 8)] + [xf[1, h, rows], high]
+                for v, x0 in ((below, 0), (above, 6)):
+                    d = [v[i + 1] - v[i] for i in range(5)]
+                    half = [0.5 * minmod(d[i], d[i + 1]) for i in range(4)]
+                    face = [jnp.where(xpos, v[i + 1] + half[i], v[i + 2] - half[i + 1]) for i in range(3)]
+                    for x in range(2):
+                        acc[x0 + x, h, rows] += step_x * (face[x + 1] - face[x])
+        return 0
+
+    lax.fori_loop(0, 16, x_outer, 0)
+    lax.fori_loop(0, 4, lambda i, _: (layer_sums(i + 4 * (i // 2)), 0)[1], 0)
 
     scatter = [remote(mom.at[(grp + o) % 8], rs.at[o], SCAT + o, peer(o)) for o in range(1, 8)]
     for cp in scatter:
@@ -284,14 +312,6 @@
         return 0
 
     lax.fori_loop(0, 8, gather_wall, 0)
-    pre[0] = sums(weight, flat(wm))
-    early = remote(pre.at[0], pre.at[1], PRE, mirror)
-    early.start()
-    load_nu.wait()
-    nu_main = spread(nu[grp], 16)
-    nu_wall = spread(nu[...].reshape(128, 16), 2)
-    basis = basis_table()
-
     total = mom[grp]
     for cp in scatter:
         cp.wait_recv()
@@ -300,13 +320,17 @@
     zr[0] = total
     cross = remote(zr.at[0], zr.at[1], CROSS, across)
     cross.start()
+    pl.when(late)(start_wall)
 
     cross.wait_recv()
-    rows = cell_values(total + zr[1], nu_main)
-    par[grp] = jnp.concatenate(list(rows) + [jnp.zeros((7, 256), F32)], axis=0)
-    gather = [remote(par.at[grp], par.at[grp], GATH + o, peer(o)) for o in range(1, 8)]
+    total = total + zr[1]
+    own = pl.ds(pl.multiple_of(grp * 16, 16), 16)
+    for h in range(2):
+        par[h, own, :] = total[:, h * 128 : h * 128 + 128]
+    gather = [remote(par.at[:, own, :], par.at[:, own, :], GATH + o, peer(o)) for o in range(1, 8)]
     for cp in gather:
         cp.start()
+
     for cp in wall:
         cp.wait_recv()
     step_wall = -DT * UNIT * jnp.abs(vz)
@@ -327,9 +351,7 @@
 
     lax.fori_loop(0, 8, wall_pass, 0)
     plus_part, minus_part = flat(dp), flat(dm)
-    early.wait_recv()
-    part = sums(sum_weights(jnp.abs(vz)), plus_part) + sums(sum_weights(-jnp.abs(vz)), minus_part)
-    cast[0] = part + (pre[0] + pre[1])
+    cast[0] = sums(sum_weights(jnp.abs(vz)), plus_part) + sums(sum_weights(-jnp.abs(vz)), minus_part)
     casts = [remote(cast.at[0], cast.at[o], CAST + o, peer(o)) for o in range(1, 8)]
     for cp in casts:
         cp.start()
@@ -338,23 +360,34 @@
     for cp in gather:
         cp.wait_recv()
 
+    def strided(k):
+        return jnp.concatenate([par[h, pl.ds(k, 8, stride=16), :] for h in range(2)], axis=1)
+
+    for k, row in enumerate(cell_values([strided(k) for k in range(16)], freq[...])):
+        vals[k] = row
+
     def main_relax(x, _):
-        table = par[x]
-        out[x] = relax([table[k : k + 1] for k in range(9)], basis, joined(acc, x), vz)
+        out[x] = relax([vals[k, pl.ds(x, 1), :] for k in range(9)], basis, joined(acc, x), vz)
         return 0
 
     lax.fori_loop(0, 8, main_relax, 0)
 
+    r, c = (lax.broadcasted_iota(jnp.int32, (256, 32), d) for d in range(2))
+    pick = jnp.where(r == (c // 2) * 16 + c % 2, 1.0, 0.0)
+    wall_sums = []
+    for x in range(8):
+        layer = jnp.concatenate([par[h, x * 16 : x * 16 + 16, :] for h in range(2)], axis=1)
+        wall_sums.append(jnp.dot(layer, pick, precision=lax.Precision.HIGHEST, preferred_element_type=F32))
+    total = jnp.concatenate(wall_sums, axis=1)
     for cp in casts:
         cp.wait_recv()
-    total = cast[0]
-    for o in range(1, 8):
+    for o in range(8):
         total = total + cast[o]
-    fixed = relax(cell_values(total, nu_wall), basis, beside, vz)
+    fixed = relax(cell_values([total[k : k + 1] for k in range(16)], nu_wall), basis, beside, vz)
     for x in range(8):
         for k in range(16):
             out[x, k * 16 : k * 16 + 2, :] = fixed[x * 32 + k * 2 : x * 32 + k * 2 + 2]
-    for cp in halo + wall + scatter + [cross, early] + gather + casts:
+    for cp in halo + wall + scatter + [cross] + gather + casts:
         cp.wait_send()
 
 
@@ -378,11 +411,12 @@
             pltpu.VMEM((8, 16, 256), F32),
             pltpu.VMEM((8, 16, 256), F32),
             pltpu.VMEM((2, 16, 256), F32),
-            pltpu.VMEM((8, 16, 256), F32),
+            pltpu.VMEM((2, 128, 128), F32),
+            pltpu.VMEM((9, 8, 256), F32),
+            pltpu.VMEM((8, 256), F32),
             pltpu.VMEM((2, 8, 32, 128), F32),
             pltpu.VMEM((2, 8, 32, 128), F32),
             pltpu.VMEM((2, 8, 32, 128), F32),
-            pltpu.VMEM((2, 16, 256), F32),
             pltpu.VMEM((8, 16, 256), F32),
             pltpu.SemaphoreType.DMA((COPIES,)),
             pltpu.SemaphoreType.DMA((COPIES,)),

time: 75 us -> 70.6 us (0.941)
  the two profiles are of different devices: /device:TPU:1 before, /device:TPU:193 now
where the time goes in v3:
time: 70.6 us; the launch traced here: 70.5 us
  Pallas kernels  69.2 us (98%)
  local copies, waits for them, and re-layouts  1.32 us (2%)
    pallas_call x1, Pallas kernels, shards(): pl.pallas_call(kernel, out_shape=jax.ShapeDtypeStruct((8, 256, 256), F32)...  69.2 us

profile of v3, /device:TPU:193, one launch (start us, length us, event | category | flops | bytes accessed | tf_op | source)
XLA Modules:
  0.0 70.5 jit_solution(15820037139454320545)
XLA Ops:
  0.0 69.2 %shard_map.28 = f32[8,256,256]{2,1,0:T(8,128)S(1)} custom-call(f32[8,256,256]{2,1,0:T(8,128)} %bitcast.3, f32[8,16,16]{2,1,0:T(8,128)} %nu_hbm.1), custom_call_target="tpu_custom_call" | custom-call | flops 100000000 | bytes 4194304 | tf_op jit(solution)/shard_map/pallas_call | solution.py:397
  69.2 1.3 %copy.4 = f32[1,8,16,16,256]{4,3,2,1,0:T(8,128)} copy(f32[1,8,16,16,256]{4,3,2,1,0:T(8,128)S(1)} %bitcast.2) | data formatting | bytes 4194304

commit v4 on v3

--- a/solution.py
+++ b/solution.py
@@ -374,11 +374,9 @@
 
     r, c = (lax.broadcasted_iota(jnp.int32, (256, 32), d) for d in range(2))
     pick = jnp.where(r == (c // 2) * 16 + c % 2, 1.0, 0.0)
-    wall_sums = []
-    for x in range(8):
-        layer = jnp.concatenate([par[h, x * 16 : x * 16 + 16, :] for h in range(2)], axis=1)
-        wall_sums.append(jnp.dot(layer, pick, precision=lax.Precision.HIGHEST, preferred_element_type=F32))
-    total = jnp.concatenate(wall_sums, axis=1)
+    every = jnp.concatenate([par[0], par[1]], axis=1)
+    picked = jnp.dot(every, pick, precision=lax.Precision.HIGHEST, preferred_element_type=F32)
+    total = jnp.concatenate([picked[x * 16 : x * 16 + 16] for x in range(8)], axis=1)
     for cp in casts:
         cp.wait_recv()
     for o in range(8):

time: 70.6 us -> 70.4 us (level)
  no operation moved by 1% of the time
where the time goes in v4:
time: 70.4 us; the launch traced here: 70.2 us
  Pallas kernels  68.9 us (98%)
  local copies, waits for them, and re-layouts  1.32 us (2%)
    pallas_call x1, Pallas kernels, shards(): pl.pallas_call(kernel, out_shape=jax.ShapeDtypeStruct((8, 256, 256), F32)...  68.9 us

profile of v4, /device:TPU:193, one launch (start us, length us, event | category | flops | bytes accessed | tf_op | source)
XLA Modules:
  0.0 70.2 jit_solution(15319988074518744890)
XLA Ops:
  0.0 68.9 %shard_map.28 = f32[8,256,256]{2,1,0:T(8,128)S(1)} custom-call(f32[8,256,256]{2,1,0:T(8,128)} %bitcast.3, f32[8,16,16]{2,1,0:T(8,128)} %nu_hbm.1), custom_call_target="tpu_custom_call" | custom-call | flops 100000000 | bytes 4194304 | tf_op jit(solution)/shard_map/pallas_call | solution.py:395
  68.9 1.3 %copy.4 = f32[1,8,16,16,256]{4,3,2,1,0:T(8,128)} copy(f32[1,8,16,16,256]{4,3,2,1,0:T(8,128)S(1)} %bitcast.2) | data formatting | bytes 4194304
